TPU v7x, 32 devices: a whole 2x2x4 slice. The times are simulated.
32 devices in a mesh: groups: 2 (over y), row: 4 (over x, core), col: 4 (over z).
Axes of the slice: x: 2, y: 2, z: 4, core: 2. Of those that a mesh axis runs over, the one named last changes fastest.
Arguments:
- pair_map: bfloat16 [192, 96, 128], P(('groups', 'row'), 'col'), parts along dimension 0, may hold values from -6 to 6
- cotangent: bfloat16 [192, 96, 128], P(('groups', 'row'), 'col'), parts along dimension 0, may hold values from -6 to 6
- residue_mask: int32 [192], P('groups'), parts along dimension 0, may hold values from 0 to 1, as said below
- gain_in: float32 [128], replicated, may hold values from 0.25 to 1.75
- w_in: bfloat16 [128, 640], replicated, may hold values from -0.5 to 0.5
- gain_mid: float32 [128], replicated, may hold values from 0.25 to 1.75
- w_out: bfloat16 [128, 128], replicated, may hold values from -0.5 to 0.5
- gain_trans: float32 [128], replicated, may hold values from 0.25 to 1.75
- w_up: bfloat16 [128, 512], replicated, may hold values from -0.5 to 0.5
- w_down: bfloat16 [512, 128], replicated, may hold values from -0.25 to 0.25
Outputs:
- updated: bfloat16 [192, 96, 128], P(('groups', 'row'), 'col'), parts along dimension 0
- gradient: bfloat16 [192, 96, 128], P(('groups', 'row'), 'col'), parts along dimension 0
There are 2 independent parts, one for each index of `groups`. A program takes and returns all parts, laid end to end along the dimension named above; an argument that names none is the same for every part. Nothing has to cross between parts.
Inputs may be any that keep to these rules, and one draw needn't show every extreme that they name: `residue_mask`: the complex is 4 slots of 24 residues each; in every slot the present residues come first, at least 3/5 of the slot (rounded down) and never the whole slot.
All inputs are finite; a program needn't handle non-finite values.
Results may differ from a plain program's by a relative error of at most 0.019.
The roundings to bfloat16 on the way count: a program that leaves them out, or rounds other values in their place, can miss the bound.
Values may be sent and summed in bfloat16 or wider, within the bound.
A program may use at most 64 MiB of HBM per device.

v0:
```python
import jax
import jax.numpy as jnp
from jax import lax
from jax.sharding import PartitionSpec as P

epsilon = 1e-05


def spread_2(block, axis, owner):
    block = jnp.where(lax.axis_index(axis) == owner, block, jnp.zeros_like(block))
    return lax.psum(block, axis)


def layer_norm(values, gain_vec):
    centred = values - jnp.mean(values, axis=-1, keepdims=True)
    spread = jnp.mean(centred * centred, axis=-1, keepdims=True)
    return centred * lax.rsqrt(spread + epsilon) * gain_vec


def project_in(pair_vals, row_mask, col_mask, gain_in, w_in):
    inner_width = (w_in.shape[1] - pair_vals.shape[-1]) // 4
    normed = layer_norm(pair_vals, gain_in).astype(jnp.bfloat16)
    projected = jnp.dot(normed, w_in, preferred_element_type=jnp.float32)
    pair_mask = row_mask[:, None, None] * col_mask[None, :, None]
    left_proj = (
        pair_mask
        * jax.nn.sigmoid(projected[..., inner_width : 2 * inner_width])
        * projected[..., :inner_width]
    )
    right_proj = (
        pair_mask
        * jax.nn.sigmoid(projected[..., 3 * inner_width : 4 * inner_width])
        * projected[..., 2 * inner_width : 3 * inner_width]
    )
    gate_vals = jax.nn.sigmoid(projected[..., 4 * inner_width :])
    return (left_proj, right_proj, gate_vals)


def project_out(combined, gate_vals, pair_vals, gain_mid, w_out):
    mixed_norm = layer_norm(combined, gain_mid).astype(jnp.bfloat16)
    return pair_vals + gate_vals * jnp.dot(mixed_norm, w_out, preferred_element_type=jnp.float32)


def transition(carried, gain_trans, w_up, w_down):
    lifted = layer_norm(carried, gain_trans).astype(jnp.bfloat16)
    hidden_units = jax.nn.relu(jnp.dot(lifted, w_up, preferred_element_type=jnp.float32)).astype(
        jnp.bfloat16
    )
    return carried + jnp.dot(hidden_units, w_down, preferred_element_type=jnp.float32)


def shards(
    pair_map, cotangent, residue_mask, gain_in, w_in, gain_mid, w_out, gain_trans, w_up, w_down
):
    tile_size = pair_map.shape[0]
    row_mask = lax.dynamic_slice_in_dim(
        residue_mask, lax.axis_index("row") * tile_size, tile_size
    ).astype(jnp.float32)
    col_mask = lax.dynamic_slice_in_dim(
        residue_mask, lax.axis_index("col") * tile_size, tile_size
    ).astype(jnp.float32)
    pair_vals = pair_map.astype(jnp.float32)

    def project_entry(values):
        return project_in(values, row_mask, col_mask, gain_in, w_in)

    (left_proj, right_proj, gate_vals), entry_back = jax.vjp(project_entry, pair_vals)
    left_half = left_proj.astype(jnp.bfloat16)
    right_half = right_proj.astype(jnp.bfloat16)
    left_rows, right_own = (
        lax.all_gather(left_half, "col", axis=1, tiled=True),
        lax.all_gather(right_half, "col", axis=1, tiled=True),
    )
    right_rows = spread_2(right_own, "row", lax.axis_index("col"))
    combined = jnp.einsum("ikh,jkh->ijh", left_rows, right_rows, preferred_element_type=jnp.float32)

    def project_exit(comb_in, gate_in, values):
        return project_out(comb_in, gate_in, values, gain_mid, w_out)

    sectioned, exit_back = jax.vjp(project_exit, combined, gate_vals, pair_vals)
    carried = lax.optimization_barrier(sectioned.astype(jnp.bfloat16)).astype(jnp.float32)

    def transition_step(values):
        return transition(values, gain_trans, w_up, w_down)

    result, step_back = jax.vjp(transition_step, carried)
    updated = result.astype(jnp.bfloat16)
    (d_carried,) = step_back(cotangent.astype(jnp.float32))
    d_combined, d_gate, d_direct = exit_back(d_carried)
    d_comb_half = d_combined.astype(jnp.bfloat16)
    grad_rows = lax.all_gather(d_comb_half, "col", axis=1, tiled=True)
    right_back = lax.all_gather(right_half, "row", axis=0, tiled=True)
    d_left = jnp.einsum("ijh,jkh->ikh", grad_rows, right_back, preferred_element_type=jnp.float32)
    grad_cols = lax.all_to_all(grad_rows, "row", split_axis=1, concat_axis=0, tiled=True)
    left_cols = lax.all_gather(left_half, "row", axis=0, tiled=True)
    d_right = jnp.einsum("ijh,ikh->jkh", grad_cols, left_cols, preferred_element_type=jnp.float32)
    (d_entry,) = entry_back((d_left, d_right, d_gate))
    return (updated, (d_entry + d_direct).astype(jnp.bfloat16))


def solution(mesh):
    in_specs = (
        P(("groups", "row"), "col", None),
        P(("groups", "row"), "col", None),
        P("groups"),
        P(),
        P(),
        P(),
        P(),
        P(),
        P(),
        P(),
    )
    out_specs = (P(("groups", "row"), "col", None), P(("groups", "row"), "col", None))
    return jax.shard_map(shards, mesh=mesh, in_specs=in_specs, out_specs=out_specs, check_vma=False)
```

profile of v0, /device:TPU:0, one launch (start us, length us, event | category | flops | bytes accessed | tf_op | source)
XLA Modules:
  0.0 132.9 jit_solution(1259945824661562640)
XLA Ops:
  7.2 1.1 convert_reduce_fusion.2
  8.3 1.2 fusion.38
  9.5 0.8 dynamic-slice_convert_fusion.1
  10.4 1.4 %fusion.63 = f32[24,24,640]{2,1,0:T(8,128)S(1)} fusion(bf16[128,640]{1,0:T(8,128)(2,1)S(1)} %copy-done, bf16[24,24,128]{2,1,0:T(8,128)(2,1)} %param.10, f32[128]{0:T(128)} %param.13, f32[24,24]{1,0:T(8,128)S(1)} %fusion.88, f32[24,24]{1,0:T(8,128)S(1)} %broadcast_multiply_fusion.3), kind=kOutput, calls=%fused_computation.92 | convolution fusion | flops 94740480 | bytes 1790976 | tf_op jit(solution)/shard_map/jvp()/dot_general | solution.py:23
  12.1 18.3 %all_gather.15 = bf16[24,96,128]{2,1,0:T(8,128)(2,1)S(1)} all-gather(bf16[24,24,128]{2,1,0:T(8,128)(2,1)S(1)} %get-tuple-element.11), channel_id=1, replica_groups=mesh['groups'=2,'row'=4,'col'=4] {'col'}, dimensions={1}, use_global_device_ids=true | all-gather | bytes 737280 | tf_op jit(solution)/shard_map/all_gather | solution.py:72
  30.4 0.9 broadcast_select_fusion
  31.3 16.6 %all_gather.16 = bf16[24,96,128]{2,1,0:T(8,128)(2,1)S(1)} all-gather(bf16[24,24,128]{2,1,0:T(8,128)(2,1)S(1)} %get-tuple-element.10), channel_id=1, replica_groups=mesh['groups'=2,'row'=4,'col'=4] {'col'}, dimensions={1}, use_global_device_ids=true | all-gather | bytes 737280 | tf_op jit(solution)/shard_map/all_gather | solution.py:71
  47.9 7.5 %all_gather.17 = bf16[96,24,128]{2,1,0:T(8,128)(2,1)S(1)} all-gather(bf16[24,24,128]{2,1,0:T(8,128)(2,1)S(1)} %get-tuple-element.10), channel_id=1, replica_groups=mesh['groups'=2,'row'=4,'col'=4] {'row'}, dimensions={0}, use_global_device_ids=true | all-gather | bytes 737280 | tf_op jit(solution)/shard_map/all_gather | solution.py:95
  55.4 1.3 copy.103
  56.7 1.4 %copy.116 = bf16[96,24,128]{0,1,2:T(8,128)(2,1)} copy(bf16[96,24,128]{2,1,0:T(8,128)(2,1)S(1)} %all_gather.17) | data formatting | bytes 1179648 | tf_op jit(solution)/shard_map/all_gather | solution.py:95
  58.1 9.8 %all_gather.19 = bf16[96,24,128]{2,1,0:T(8,128)(2,1)S(1)} all-gather(bf16[24,24,128]{2,1,0:T(8,128)(2,1)S(1)} %get-tuple-element.11), channel_id=1, replica_groups=mesh['groups'=2,'row'=4,'col'=4] {'row'}, dimensions={0}, use_global_device_ids=true | all-gather | bytes 737280 | tf_op jit(solution)/shard_map/all_gather | solution.py:92
  67.9 1.5 %copy.119 = bf16[96,24,128]{0,1,2:T(8,128)(2,1)} copy(bf16[96,24,128]{2,1,0:T(8,128)(2,1)S(1)} %all_gather.19) | data formatting | bytes 1179648 | tf_op jit(solution)/shard_map/all_gather | solution.py:92
  69.4 2.3 %copy.102 = bf16[24,96,128]{1,0,2:T(8,128)(2,1)} copy(bf16[24,96,128]{2,1,0:T(8,128)(2,1)} %all-reduce.7.cloned.1.call-done) | data formatting | bytes 1179648 | tf_op jit(solution)/shard_map/psum | solution.py:11
  71.7 2.5 %bitcast_reduce_fusion = (f32[24,24]{0,1:T(8,128)}, f32[128,24,24]{2,1,0:T(8,128)S(1)}) fusion(bf16[24,96,128]{1,0,2:T(8,128)(2,1)} %copy.102, bf16[24,96,128]{1,0,2:T(8,128)(2,1)} %copy.103), kind=kOutput, calls=%fused_computation | convolution fusion | flops 14228928 | bytes 1476864 | tf_op jit(solution)/shard_map/ikh,jkh->ijh/dot_general | solution.py:75
  75.8 1.3 fusion.42
  77.6 1.2 convert_reduce_fusion
  79.1 1.7 %fusion.46 = (f32[24,24]{1,0:T(8,128)S(1)}, f32[24,24,128]{2,1,0:T(8,128)S(1)}) fusion(bf16[24,24,128]{2,1,0:T(8,128)(2,1)S(1)} %get-tuple-element.16, f32[24,24]{1,0:T(8,128)S(1)} %broadcast_multiply_fusion.1, f32[128]{0:T(128)S(1)} %copy-done.11, bf16[128,512]{1,0:T(8,128)(2,1)S(1)} %copy-done.8, pred[24,24,512]{2,1,0:T(8,128)(4,1)S(1)} %and_convert_fusion, ...), kind=kOutput, calls=%fused_computation.59 | convolution fusion | flops 152395200 | bytes 1152000 | tf_op jit(solution)/shard_map/transpose(jvp())/dot_general | solution.py:46
  81.2 1.1 fusion.47
  83.5 17.4 %all_gather.18 = bf16[24,96,128]{2,1,0:T(8,128)(2,1)S(1)} all-gather(bf16[24,24,128]{2,1,0:T(8,128)(2,1)S(1)} %add_convert_fusion.1), channel_id=1, replica_groups=mesh['groups'=2,'row'=4,'col'=4] {'col'}, dimensions={1}, use_global_device_ids=true | all-gather | bytes 737280 | tf_op jit(solution)/shard_map/all_gather | solution.py:91
  100.9 1.0 copy.113
  101.9 1.3 copy.120
  103.2 4.3 %all-to-all-start = ((bf16[24,96,128]{2,0,1:T(8,128)(2,1)}), bf16[24,96,128]{2,0,1:T(8,128)(2,1)}, u32[]{:S(2)}, u32[]{:S(2)}) async-start(bf16[24,96,128]{2,0,1:T(8,128)(2,1)} %copy.113), calls=%async_computation | async-start | bytes 1179648 | tf_op jit(solution)/shard_map/all_to_all | solution.py:94
  107.5 1.9 %fusion.98 = f32[128,24,24]{2,1,0:T(8,128)S(1)} fusion(bf16[96,24,128]{0,1,2:T(8,128)(2,1)} %copy.119, bf16[24,96,128]{1,0,2:T(8,128)(2,1)} %copy.120), kind=kOutput, calls=%fused_computation.136 | convolution fusion | flops 14155776 | bytes 1474560 | tf_op jit(solution)/shard_map/ijh,jkh->ikh/dot_general | solution.py:93
  109.5 1.2 copy.121
  110.7 2.1 %fusion.13 = bf16[24,24,128]{2,1,0:T(8,128)(2,1)} fusion(bf16[24,24,512]{2,1,0:T(8,128)(2,1)} %get-tuple-element.19, bf16[24,24,128]{2,1,0:T(8,128)(2,1)S(1)} %get-tuple-element.16, bf16[512,128]{1,0:T(8,128)(2,1)S(1)} %copy-done.9), kind=kOutput, calls=%fused_computation.19 | convolution fusion | flops 76603392 | bytes 1015808 | tf_op jit(solution)/shard_map/jvp()/dot_general | solution.py:49
  112.7 4.2 %all-to-all-done = bf16[24,96,128]{2,0,1:T(8,128)(2,1)} async-done(((bf16[24,96,128]{2,0,1:T(8,128)(2,1)}), bf16[24,96,128]{2,0,1:T(8,128)(2,1)}, u32[]{:S(2)}, u32[]{:S(2)}) %all-to-all-start) | async-done | bytes 589856 | tf_op jit(solution)/shard_map/all_to_all | solution.py:94
  117.0 1.1 copy.115
  118.1 1.5 %copy.117 = bf16[96,24,128]{0,1,2:T(8,128)(2,1)} copy(bf16[96,24,128]{2,1,0:T(8,128)(2,1)S(1)} %bitcast.77) | data formatting | bytes 1179648 | tf_op jit(solution)/shard_map/all_to_all | solution.py:94
  119.6 1.9 %fusion.97 = f32[128,24,24]{2,1,0:T(8,128)S(1)} fusion(bf16[96,24,128]{0,1,2:T(8,128)(2,1)} %copy.116, bf16[96,24,128]{0,1,2:T(8,128)(2,1)} %copy.117), kind=kOutput, calls=%fused_computation.135 | convolution fusion | flops 14155776 | bytes 1474560 | tf_op jit(solution)/shard_map/ijh,ikh->jkh/dot_general | solution.py:96
  121.5 1.2 copy.118
  122.7 1.3 bitcast_multiply_fusion.3
  125.0 1.0 add_convert_fusion
  (55 shorter events, 5.1 us)
Async XLA Ops:
  7.2 3.3 %copy-start = (bf16[128,640]{1,0:T(8,128)(2,1)S(1)}, bf16[128,640]{1,0:T(8,128)(2,1)}, u32[]{:S(2)}) copy-start(bf16[128,640]{1,0:T(8,128)(2,1)} %param.14) | copy-start | bytes 491524
  7.2 62.2 %all-reduce.7.cloned.1.call-start = ((), (), s32[]{:S(2)}) async-start(), calls=%async_computation.1 | async-start | bytes 1179648 | tf_op jit(solution)/shard_map/psum | solution.py:11
  74.7 2.9 %copy-start.8 = (bf16[128,512]{1,0:T(8,128)(2,1)S(1)}, bf16[128,512]{1,0:T(8,128)(2,1)}, u32[]{:S(2)}) copy-start(bf16[128,512]{1,0:T(8,128)(2,1)} %param.18) | copy-start | bytes 393220
  74.7 2.9 %copy-start.11 = (f32[128]{0:T(128)S(1)}, f32[128]{0:T(128)}, u32[]{:S(2)}) copy-start(f32[128]{0:T(128)} %param.17) | copy-start | bytes 1540
  77.1 2.0 %copy-start.6 = (bf16[24,24,128]{2,1,0:T(8,128)(2,1)S(1)}, bf16[24,24,128]{2,1,0:T(8,128)(2,1)}, u32[]{:S(2)}) copy-start(bf16[24,24,128]{2,1,0:T(8,128)(2,1)} %param.11) | copy-start | bytes 442372
  80.8 1.5 %copy-start.10 = (bf16[128,128]{1,0:T(8,128)(2,1)S(1)}, bf16[128,128]{1,0:T(8,128)(2,1)}, u32[]{:S(2)}) copy-start(bf16[128,128]{1,0:T(8,128)(2,1)} %param.16) | copy-start | bytes 98308
  80.8 1.5 %copy-start.12 = (f32[128]{0:T(128)S(1)}, f32[128]{0:T(128)}, u32[]{:S(2)}) copy-start(f32[128]{0:T(128)} %param.15) | copy-start | bytes 1540
  82.3 0.8 copy-start.3
  103.2 13.8 %all-to-all-start = ((bf16[24,96,128]{2,0,1:T(8,128)(2,1)}), bf16[24,96,128]{2,0,1:T(8,128)(2,1)}, u32[]{:S(2)}, u32[]{:S(2)}) async-start(bf16[24,96,128]{2,0,1:T(8,128)(2,1)} %copy.113), calls=%async_computation | async-start | bytes 1179648 | tf_op jit(solution)/shard_map/all_to_all | solution.py:94
  109.5 1.2 copy-start.9
  121.5 1.2 copy-start.2
  122.7 1.3 copy-start.1
  122.7 1.3 copy-start.5
  122.7 1.3 copy-start.7
  124.0 1.0 copy-start.4
Sparse Core Ops, SparseCore 0:
  31.4 35.8 all-reduce.6
where the time goes:
time: 133 us
  blocking collectives  69.7 us (52%)
  local copies, waits for them, and re-layouts  15.1 us (11%)
  matrix products  14.9 us (11%)
  between operations  14.4 us (11%)
  other arithmetic  10.2 us (8%)
  starting transfers between devices  4.36 us (3%)
  waiting for transfers between devices  4.25 us (3%)
    all_gather x1, blocking collectives, shards(): lax.all_gather(right_half, 'col', axis=1, tiled=True)  18.3 us
    all_gather x1, blocking collectives, shards(): grad_rows = lax.all_gather(d_comb_half, 'col', axis=1, tiled=True)  17.4 us
    all_gather x1, blocking collectives, shards(): lax.all_gather(left_half, 'col', axis=1, tiled=True)  16.6 us
    all_gather x1, blocking collectives, shards(): right_back = lax.all_gather(right_half, 'row', axis=0, tiled=True)  9.77 us
    all_gather x1, blocking collectives, shards(): left_cols = lax.all_gather(left_half, 'row', axis=0, tiled=True)  7.51 us
    all_to_all x1, starting transfers between devices, shards(): lax.all_to_all(grad_rows, 'row', split_axis=1, concat_axis=0, tiled=True)  4.32 us
    all_to_all x1, waiting for transfers between devices, shards(): lax.all_to_all(grad_rows, 'row', split_axis=1, concat_axis=0, tiled=True)  4.23 us
    dot_general x2, matrix products, transition(): jnp.dot(lifted, w_up, preferred_element_type=jnp.float32)  2.9 us
  transfers between devices with their start and end apart: 2, of which 1 were waited for; matrix products, arithmetic and copies ran while one was open for 7% of the time, Pallas kernels for 0%

commit v1 on v0

v1 whole, which is shorter than its diff:
```python
import functools

import jax
import jax.numpy as jnp
from jax import lax
from jax.experimental import pallas as pl
from jax.experimental.pallas import tpu as pltpu
from jax.sharding import PartitionSpec as P

epsilon = 1e-05
PIECES = 4
MESH = pl.DeviceIdType.MESH
F32 = jnp.float32
BF16 = jnp.bfloat16


def nn(a, b):
    return jnp.dot(a, b, preferred_element_type=F32)


def nt(a, b):
    return lax.dot_general(a, b, (((1,), (1,)), ((), ())), preferred_element_type=F32)


def ln(values):
    centred = values - jnp.mean(values, axis=-1, keepdims=True)
    inv = lax.rsqrt(jnp.mean(centred * centred, axis=-1, keepdims=True) + epsilon)
    return centred * inv, inv


def ln_back(d_hat, hat, inv):
    return inv * (
        d_hat
        - jnp.mean(d_hat, axis=-1, keepdims=True)
        - hat * jnp.mean(d_hat * hat, axis=-1, keepdims=True)
    )


def sigmoid(v):
    return jax.nn.sigmoid(v)


def products(t, a_ref, a_row, b_ref, b_rows, out_ref, add):
    def block(n, _):
        acc = [None] * 8
        for s in range(t):
            b = b_ref[b_rows(s), :]
            for u in range(8):
                term = a_ref[pl.ds(a_row(n * 8 + u, s), 1), :] * b
                acc[u] = term if acc[u] is None else acc[u] + term
        for u in range(8):
            at = pl.ds(pl.multiple_of((n * 8 + u) * t, 8), t)
            out_ref[at, :] = out_ref[at, :] + acc[u] if add else acc[u]
        return 0

    lax.fori_loop(0, t // 8, block, 0)


def kernel(
    peers, t, step,
    mask_ref, x_ref, cot_ref, gin_ref, win_ref, gmid_ref, wout_ref, gtr_ref, wup_ref, wdn_ref,
    up_ref, grad_ref,
    r_all, l_all, rt, l_row, dc_row, dc_col,
    mask_v, hat_v, inv_v, proj_v, own_v, a_v, b_v, dleft_v, dright_v, dcar_v, dgate_v,
    s_send, s_recv,
):
    row, col = lax.axis_index("row"), lax.axis_index("col")
    rows = t * t
    c = x_ref.shape[-1]
    chunks = [pl.ds(n, step) for n in range(0, rows, step)]

    barrier = pltpu.get_barrier_semaphore()
    for s in range(1, peers):
        pl.semaphore_signal(
            barrier, inc=1, device_id={"row": lax.rem(row + s, peers)}, device_id_type=MESH
        )
        pl.semaphore_signal(
            barrier, inc=1, device_id={"col": lax.rem(col + s, peers)}, device_id_type=MESH
        )

    def copy(kind, src, dst, slot, axis, peer, lane=None):
        return pltpu.make_async_remote_copy(
            src_ref=src, dst_ref=dst,
            send_sem=s_send.at[kind if lane is None else lane, peer if lane is None else slot],
            recv_sem=s_recv.at[kind, slot], device_id={axis: peer}, device_id_type=MESH,
        )

    size = rows // PIECES
    mine = lax.rem(row, PIECES)
    base = row - mine

    def part(ref, slot, p):
        return ref.at[slot, pl.ds(pl.multiple_of(p * size, 16), size)]

    def first(src, peer, p):
        return copy(0, part(r_all, src, p), part(r_all, src, p), src, "row", peer)

    def left_over_rows(src, peer):
        return copy(1, l_all.at[src], l_all.at[src], src, "row", peer)

    def to_column(src, slot, peer):
        return copy(2, part(r_all, src, mine), part(rt, slot, mine), slot, "col", peer)

    def in_set(slot, m, p, peer):
        d = part(rt, slot, p)
        return copy(2 + m, d, d, slot, "row", peer, lane=2 + m)

    def rest(src, m, p, peer):
        d = part(r_all, src, p)
        return copy(5 + m, d, d, src, "row", peer)

    def dc_over_rows(src, slot, peer):
        return copy(9, dc_row.at[src], dc_col.at[slot], slot, "row", peer)

    def along(kind, ref, tile, n, up):
        d = ref.at[tile, chunks[n]]
        peer = col + 1 if up else col - 1
        return copy(kind + n, d, d, tile, "col", peer, lane=kind + n + (0 if up else 6))

    def pass_on(kind, ref, tile, n, up):
        @pl.when((col + 1 < peers) if up else (col > 0))
        def _():
            along(kind, ref, tile, n, up).start()

    def forward(kind, ref, s):
        for n in range(len(chunks)):
            for up in (True, False):
                tile = col - s if up else col + s

                @pl.when((tile >= 0) if up else (tile < peers))
                def _():
                    along(kind, ref, tile, n, not up).wait_recv()
                    pass_on(kind, ref, tile, n, up)

    def both(s, body):
        @pl.when(col - s >= 0)
        def _():
            body(col - s)

        @pl.when(col + s < peers)
        def _():
            body(col + s)

    def start_rest():
        def per_peer(s, _):
            peer = lax.rem(row + s, peers)
            for m in range(1, PIECES):
                rest(row, m, lax.rem(lax.rem(peer, PIECES) + m, PIECES), peer).start()
            return 0

        lax.fori_loop(1, peers, per_peer, 0)

    def wait_rest(src):
        for m in range(1, PIECES):
            rest(src, m, lax.rem(mine + m, PIECES), src).wait_recv()

    at_k = lax.broadcasted_iota(jnp.int32, (t, c), 0)
    m_k = jnp.zeros((t, c), F32)
    for k in range(t):
        m_k = jnp.where(at_k == k, mask_ref[col * t + k].astype(F32), m_k)
    for i in range(t):
        mask_v[i * t : (i + 1) * t, :] = m_k * mask_ref[row * t + i].astype(F32)

    for at in chunks:
        hat, inv = ln(x_ref[at, :].astype(F32))
        hat_v[at, :] = hat
        inv_v[at, :] = jnp.broadcast_to(inv, hat.shape)
        normed = (hat * gin_ref[...]).astype(BF16)
        pr = nn(normed, win_ref[:, 2 * c : 4 * c])
        gate = sigmoid(pr[:, c:])
        proj_v[at, 2 * c : 3 * c] = pr[:, :c]
        proj_v[at, 3 * c : 4 * c] = gate
        r_all[row, at, :] = (mask_v[at, :] * gate * pr[:, :c]).astype(BF16)

    pl.semaphore_wait(barrier, 2 * (peers - 1))

    def send_r(s, _):
        peer = lax.rem(row + s, peers)
        first(row, peer, lax.rem(peer, PIECES)).start()
        return 0

    lax.fori_loop(1, peers, send_r, 0)

    for n, at in enumerate(chunks):
        normed = (hat_v[at, :] * gin_ref[...]).astype(BF16)
        pr = nn(normed, win_ref[:, : 2 * c])
        gate = sigmoid(pr[:, c:])
        proj_v[at, :c] = pr[:, :c]
        proj_v[at, c : 2 * c] = gate
        left = (mask_v[at, :] * gate * pr[:, :c]).astype(BF16)
        l_row[col, at, :] = left
        for up in (True, False):
            pass_on(10, l_row, col, n, up)
        l_all[row, at, :] = left

    def piece_step(s, _):
        src = lax.rem(row - s + peers, peers)

        @pl.when(s > 0)
        def _():
            first(src, src, mine).wait_recv()

        @pl.when(src != col)
        def _():
            to_column(src, col, src).start()

        return 0

    lax.fori_loop(0, peers, piece_step, 0)

    @pl.when(row == col)
    def _():
        start_rest()

    for at in chunks:
        normed = (hat_v[at, :] * gin_ref[...]).astype(BF16)
        proj_v[at, 4 * c :] = sigmoid(nn(normed, win_ref[:, 4 * c :]))
        own_v[at, :] = jnp.zeros((step, c), F32)

    def share(slot):
        to_column(slot, slot, slot).wait_recv()
        for m in range(1, PIECES):
            in_set(slot, m, mine, base + lax.rem(mine + m, PIECES)).start()

    def combine(slot):
        @pl.when(slot == col)
        def _():
            @pl.when(row != col)
            def _():
                wait_rest(col)

            for at in chunks:
                b_v[at, :] = r_all[col, at, :].astype(F32)

        @pl.when(slot != col)
        def _():
            for m in range(1, PIECES):
                p = lax.rem(mine - m + PIECES, PIECES)
                in_set(slot, m, p, base + p).wait_recv()
            for at in chunks:
                b_v[at, :] = rt[slot, at, :].astype(F32)

        for at in chunks:
            a_v[at, :] = l_row[slot, at, :].astype(F32)
        products(t, a_v, lambda p, k: p * t + k, b_v, lambda k: pl.ds(k, t, stride=t), own_v, True)

    def forward_step(s, _):
        forward(10, l_row, s)
        both(s, share)

        @pl.when(s == 1)
        def _():
            combine(col)

        @pl.when(s > 1)
        def _():
            both(s - 1, combine)

        return 0

    lax.fori_loop(1, peers, forward_step, 0)

    @pl.when(row != col)
    def _():
        start_rest()

    def send_l(s, _):
        left_over_rows(row, lax.rem(row + s, peers)).start()
        return 0

    lax.fori_loop(1, peers, send_l, 0)
    both(peers - 1, combine)

    for n, at in enumerate(chunks):
        hat, inv = ln(own_v[at, :])
        mixed = (hat * gmid_ref[...]).astype(BF16)
        out = nn(mixed, wout_ref[...])
        gate = proj_v[at, 4 * c :]
        carried = (x_ref[at, :].astype(F32) + gate * out).astype(BF16).astype(F32)
        hat_t, inv_t = ln(carried)
        up = nn((hat_t * gtr_ref[...]).astype(BF16), wup_ref[...])
        hidden = jnp.maximum(up, 0.0).astype(BF16)
        up_ref[at, :] = (carried + nn(hidden, wdn_ref[...])).astype(BF16)
        cot = cot_ref[at, :]
        d_hidden = nt(cot, wdn_ref[...]).astype(BF16)
        d_up = jnp.where(up > 0.0, d_hidden.astype(F32), 0.0).astype(BF16)
        d_lifted = nt(d_up, wup_ref[...]).astype(BF16).astype(F32)
        d_car = cot.astype(F32) + ln_back(d_lifted * gtr_ref[...], hat_t, inv_t)
        dcar_v[at, :] = d_car
        dgate_v[at, :] = d_car * out * gate * (1.0 - gate)
        d_mixed = nt((d_car * gate).astype(BF16), wout_ref[...]).astype(BF16).astype(F32)
        dc_row[col, at, :] = ln_back(d_mixed * gmid_ref[...], hat, inv).astype(BF16)

        for up in (True, False):
            pass_on(13, dc_row, col, n, up)
        dleft_v[at, :] = jnp.zeros((step, c), F32)
        dright_v[at, :] = jnp.zeros((step, c), F32)

    def hand_on(tile):
        @pl.when(tile == row)
        def _():
            dc_col[row] = dc_row[tile]

        @pl.when(tile != row)
        def _():
            dc_over_rows(tile, row, tile).start()

    def to_left(tile):
        @pl.when((tile != row) & (tile != col))
        def _():
            wait_rest(tile)

        for at in chunks:
            a_v[at, :] = dc_row[tile, at, :].astype(F32)
            b_v[at, :] = r_all[tile, at, :].astype(F32)
        products(t, a_v, lambda p, j: p * t + j, b_v, lambda j: pl.ds(j * t, t), dleft_v, True)

    hand_on(col)

    def back_step(s, _):
        forward(13, dc_row, s)
        both(s, hand_on)

        @pl.when(s == 1)
        def _():
            to_left(col)

        @pl.when(s > 1)
        def _():
            both(s - 1, to_left)

        return 0

    lax.fori_loop(1, peers, back_step, 0)
    both(peers - 1, to_left)

    def right_step(s, _):
        src = lax.rem(row - s + peers, peers)

        @pl.when(s > 0)
        def _():
            left_over_rows(src, src).wait_recv()
            dc_over_rows(src, src, src).wait_recv()

        for at in chunks:
            a_v[at, :] = dc_col[src, at, :].astype(F32)
            b_v[at, :] = l_all[src, at, :].astype(F32)
        products(t, a_v, lambda p, i: i * t + p, b_v, lambda i: pl.ds(i * t, t), dright_v, True)
        return 0

    lax.fori_loop(0, peers, right_step, 0)

    for at in chunks:
        total = None
        for n, d_ref in ((0, dleft_v), (2 * c, dright_v)):
            value, gate = proj_v[at, n : n + c], proj_v[at, n + c : n + 2 * c]
            d = d_ref[at, :] * mask_v[at, :] * gate
            d_value = d.astype(BF16)
            d_gate = (d * value * (1.0 - gate)).astype(BF16)
            term = nt(d_value, win_ref[:, n : n + c]) + nt(d_gate, win_ref[:, n + c : n + 2 * c])
            total = term if total is None else total + term
        total = total + nt(dgate_v[at, :].astype(BF16), win_ref[:, 4 * c :])
        d_normed = total.astype(BF16).astype(F32)
        d_entry = ln_back(d_normed * gin_ref[...], hat_v[at, :], inv_v[at, :])
        grad_ref[at, :] = (d_entry + dcar_v[at, :]).astype(BF16)

    def finish(tile, _):
        @pl.when(tile != row)
        def _():
            first(row, tile, mine).wait_send()
            left_over_rows(row, tile).wait_send()
            for m in range(1, PIECES):
                rest(row, m, mine, tile).wait_send()
            dc_over_rows(tile, row, tile).wait_send()

        @pl.when(tile != col)
        def _():
            to_column(tile, col, tile).wait_send()
            for m in range(1, PIECES):
                in_set(tile, m, mine, base + lax.rem(mine + m, PIECES)).wait_send()

        for kind, ref in ((10, l_row), (13, dc_row)):
            for n in range(len(chunks)):

                @pl.when((tile <= col) & (col + 1 < peers))
                def _():
                    along(kind, ref, tile, n, True).wait_send()

                @pl.when((tile >= col) & (col > 0))
                def _():
                    along(kind, ref, tile, n, False).wait_send()

        return 0

    lax.fori_loop(0, peers, finish, 0)


def shards(
    peers, pair_map, cotangent, residue_mask, gain_in, w_in, gain_mid, w_out, gain_trans, w_up, w_down
):
    t, _, c = pair_map.shape
    rows = t * t
    step = rows // 3
    tile, tile_all = (rows, c), (peers, rows, c)
    vmem = pl.BlockSpec(memory_space=pltpu.VMEM)
    up, grad = pl.pallas_call(
        functools.partial(kernel, peers, t, step),
        out_shape=[jax.ShapeDtypeStruct(tile, BF16)] * 2,
        in_specs=[pl.BlockSpec(memory_space=pltpu.SMEM)] + [vmem] * 9,
        out_specs=[vmem] * 2,
        scratch_shapes=[pltpu.VMEM(tile_all, BF16)] * 6
        + [pltpu.VMEM(tile, F32)] * 3
        + [pltpu.VMEM((rows, w_in.shape[1]), F32)]
        + [pltpu.VMEM(tile, F32)] * 7
        + [
            pltpu.SemaphoreType.DMA((22, peers)),
            pltpu.SemaphoreType.DMA((16, peers)),
        ],
        compiler_params=pltpu.CompilerParams(
            collective_id=0, has_side_effects=True, vmem_limit_bytes=48 * 1024 * 1024
        ),
    )(
        residue_mask, pair_map.reshape(tile), cotangent.reshape(tile), gain_in[None], w_in,
        gain_mid[None], w_out, gain_trans[None], w_up, w_down,
    )
    return up.reshape(pair_map.shape), grad.reshape(pair_map.shape)


def solution(mesh):
    tiles = P(("groups", "row"), "col", None)
    in_specs = (tiles, tiles, P("groups")) + (P(),) * 7
    return jax.shard_map(
        functools.partial(shards, mesh.shape["row"]),
        mesh=mesh, in_specs=in_specs, out_specs=(tiles, tiles), check_vma=False,
    )
```

time: 133 us -> 51.6 us (0.39)
  blocking collectives: 69.7 us -> 0 us
  Pallas kernels: 0 us -> 43.3 us
  matrix products: 14.9 us -> 0 us
  between operations: 14.4 us -> 0.68 us
  other arithmetic: 10.2 us -> 0 us
  local copies, waits for them, and re-layouts: 15.1 us -> 7.29 us
  starting transfers between devices: 4.36 us -> 0 us
  waiting for transfers between devices: 4.25 us -> 0 us
    all_gather x5 -> x0, blocking collectives: 69.7 us -> none  [the longest x1 18.3 us: shards(): lax.all_gather(right_half, 'col', axis=1, tiled=True)]
    pallas_call x0 -> x1, Pallas kernels: none -> 43.3 us  [shards(): pl.pallas_call(functools.partial(kernel, peers, t, step), out_shape=[jax....]
    dot_general x10 -> x0, matrix products: 14.9 us -> none  [the longest x2 2.9 us: transition(): jnp.dot(lifted, w_up, preferred_element_type=jnp.float32)]
    unnamed x26 -> x22, local copies, waits for them, and re-layouts: 0.08 us -> 7.29 us
    all_gather x5 -> x0, local copies, waits for them, and re-layouts: 6.46 us -> none  [the longest x2 2.31 us: shards(): grad_rows = lax.all_gather(d_comb_half, 'col', axis=1, tiled=True)]
    all_to_all x1 -> x0, starting transfers between devices: 4.32 us -> none  [shards(): lax.all_to_all(grad_rows, 'row', split_axis=1, concat_axis=0, tiled=True)]
    all_to_all x1 -> x0, waiting for transfers between devices: 4.23 us -> none  [shards(): lax.all_to_all(grad_rows, 'row', split_axis=1, concat_axis=0, tiled=True)]
    reduce_sum x8 -> x0, other arithmetic: 4.13 us -> none  [the longest x5 2.42 us: layer_norm(): centred = values - jnp.mean(values, axis=-1, keepdims=True)]
  transfers between devices with their start and end apart: 2 -> 0, of which waited for: 1 -> 0; matrix products, arithmetic and copies ran while one was open for 7% -> 0% of each run, Pallas kernels for 0% -> 0%
where the time goes in v1:
time: 51.6 us; the launch traced here: 51.3 us
  Pallas kernels  43.3 us (84%)
  local copies, waits for them, and re-layouts  7.29 us (14%)
  between operations  0.68 us (1%)
    pallas_call x1, Pallas kernels, shards(): pl.pallas_call(functools.partial(kernel, peers, t, step), out_shape=[jax....  43.3 us
    unnamed x22, local copies, waits for them, and re-layouts  7.29 us

profile of v1, /device:TPU:0, one launch (start us, length us, event | category | flops | bytes accessed | tf_op | source)
XLA Modules:
  0.0 51.3 jit_solution(15070824565297489121)
XLA Ops:
  0.6 0.0 copy-start.9
  0.6 0.0 copy-start.6
  0.7 0.0 copy-start.7
  0.7 0.0 copy-start.8
  0.7 0.6 %copy-done.9 = f32[128]{0:T(128)S(1)} copy-done((f32[128]{0:T(128)S(1)}, f32[128]{0:T(128)}, u32[]{:S(2)}) %copy-start.9) | copy-done | bytes 536
  1.3 0.0 copy-done.6
  1.3 0.0 copy-done.7
  1.3 0.0 copy-done.8
  1.3 0.0 copy-start
  1.3 0.9 %copy-done = bf16[128,640]{1,0:T(8,128)(2,1)S(1)} copy-done((bf16[128,640]{1,0:T(8,128)(2,1)S(1)}, bf16[128,640]{1,0:T(8,128)(2,1)}, u32[]{:S(2)}) %copy-start) | copy-done | bytes 163864
  2.3 0.0 copy-start.1
  2.3 0.9 %copy-done.1 = bf16[24,24,128]{2,1,0:T(8,128)(2,1)S(1)} copy-done((bf16[24,24,128]{2,1,0:T(8,128)(2,1)S(1)}, bf16[24,24,128]{2,1,0:T(8,128)(2,1)}, u32[]{:S(2)}) %copy-start.1) | copy-done | bytes 147480
  3.2 0.0 copy-start.2
  3.2 0.9 %copy-done.2 = bf16[24,24,128]{2,1,0:T(8,128)(2,1)S(1)} copy-done((bf16[24,24,128]{2,1,0:T(8,128)(2,1)S(1)}, bf16[24,24,128]{2,1,0:T(8,128)(2,1)}, u32[]{:S(2)}) %copy-start.2) | copy-done | bytes 147480
  4.1 0.0 copy-start.3
  4.1 0.9 %copy-done.3 = bf16[128,512]{1,0:T(8,128)(2,1)S(1)} copy-done((bf16[128,512]{1,0:T(8,128)(2,1)S(1)}, bf16[128,512]{1,0:T(8,128)(2,1)}, u32[]{:S(2)}) %copy-start.3) | copy-done | bytes 131096
  5.0 0.0 copy-start.4
  5.0 0.9 %copy-done.4 = bf16[512,128]{1,0:T(8,128)(2,1)S(1)} copy-done((bf16[512,128]{1,0:T(8,128)(2,1)S(1)}, bf16[512,128]{1,0:T(8,128)(2,1)}, u32[]{:S(2)}) %copy-start.4) | copy-done | bytes 131096
  5.9 0.0 copy-start.5
  5.9 0.8 %copy-done.5 = bf16[128,128]{1,0:T(8,128)(2,1)S(1)} copy-done((bf16[128,128]{1,0:T(8,128)(2,1)S(1)}, bf16[128,128]{1,0:T(8,128)(2,1)}, u32[]{:S(2)}) %copy-start.5) | copy-done | bytes 32792
  6.6 43.3 %shard_map.113 = (bf16[576,128]{1,0:T(8,128)(2,1)S(1)}, bf16[576,128]{1,0:T(8,128)(2,1)S(1)}) custom-call(s32[96]{0:T(128)S(1)} %copy-done.6, bf16[576,128]{1,0:T(8,128)(2,1)S(1)} %bitcast.9, bf16[576,128]{1,0:T(8,128)(2,1)S(1)} %bitcast.10, f32[1,128]{1,0:T(1,128)S(1)} %bitcast.11, bf16[128,640]{1,0:T(8,128)(2,1)S(1)} %copy-done, f32[1,128]{1,0:T(1,128)S(1)} %bitcast.12, ...), custom_call_target="tpu_custom_call" | custom-call | tf_op jit(solution)/shard_map/pallas_call | solution.py:406
  49.9 0.7 %copy.14 = bf16[24,24,128]{2,1,0:T(8,128)(2,1)} copy(bf16[24,24,128]{2,1,0:T(8,128)(2,1)S(1)} %bitcast.8) | data formatting | bytes 294912
  50.6 0.7 %copy.15 = bf16[24,24,128]{2,1,0:T(8,128)(2,1)} copy(bf16[24,24,128]{2,1,0:T(8,128)(2,1)S(1)} %bitcast.7) | data formatting | bytes 294912
Async XLA Ops:
  0.6 0.7 %copy-start.9 = (f32[128]{0:T(128)S(1)}, f32[128]{0:T(128)}, u32[]{:S(2)}) copy-start(f32[128]{0:T(128)} %param.17) | copy-start | bytes 1540
  0.6 0.7 %copy-start.6 = (s32[96]{0:T(128)S(1)}, s32[96]{0:T(128)}, u32[]{:S(2)}) copy-start(s32[96]{0:T(128)} %mask_ref.1) | copy-start | bytes 1156
  0.7 0.7 %copy-start.7 = (f32[128]{0:T(128)S(1)}, f32[128]{0:T(128)}, u32[]{:S(2)}) copy-start(f32[128]{0:T(128)} %param.13) | copy-start | bytes 1540
  0.7 0.7 %copy-start.8 = (f32[128]{0:T(128)S(1)}, f32[128]{0:T(128)}, u32[]{:S(2)}) copy-start(f32[128]{0:T(128)} %param.15) | copy-start | bytes 1540
  1.3 0.9 %copy-start = (bf16[128,640]{1,0:T(8,128)(2,1)S(1)}, bf16[128,640]{1,0:T(8,128)(2,1)}, u32[]{:S(2)}) copy-start(bf16[128,640]{1,0:T(8,128)(2,1)} %win_ref.1) | copy-start | bytes 491524
  2.3 0.9 %copy-start.1 = (bf16[24,24,128]{2,1,0:T(8,128)(2,1)S(1)}, bf16[24,24,128]{2,1,0:T(8,128)(2,1)}, u32[]{:S(2)}) copy-start(bf16[24,24,128]{2,1,0:T(8,128)(2,1)} %param.10) | copy-start | bytes 442372
  3.2 0.9 %copy-start.2 = (bf16[24,24,128]{2,1,0:T(8,128)(2,1)S(1)}, bf16[24,24,128]{2,1,0:T(8,128)(2,1)}, u32[]{:S(2)}) copy-start(bf16[24,24,128]{2,1,0:T(8,128)(2,1)} %param.11) | copy-start | bytes 442372
  4.1 0.9 %copy-start.3 = (bf16[128,512]{1,0:T(8,128)(2,1)S(1)}, bf16[128,512]{1,0:T(8,128)(2,1)}, u32[]{:S(2)}) copy-start(bf16[128,512]{1,0:T(8,128)(2,1)} %wup_ref.1) | copy-start | bytes 393220
  5.0 0.9 %copy-start.4 = (bf16[512,128]{1,0:T(8,128)(2,1)S(1)}, bf16[512,128]{1,0:T(8,128)(2,1)}, u32[]{:S(2)}) copy-start(bf16[512,128]{1,0:T(8,128)(2,1)} %wdn_ref.1) | copy-start | bytes 393220
  5.9 0.8 %copy-start.5 = (bf16[128,128]{1,0:T(8,128)(2,1)S(1)}, bf16[128,128]{1,0:T(8,128)(2,1)}, u32[]{:S(2)}) copy-start(bf16[128,128]{1,0:T(8,128)(2,1)} %wout_ref.1) | copy-start | bytes 98308

commit v2 on v1

--- a/solution.py
+++ b/solution.py
@@ -58,8 +58,9 @@
 
 def kernel(
     peers, t, step,
-    mask_ref, x_ref, cot_ref, gin_ref, win_ref, gmid_ref, wout_ref, gtr_ref, wup_ref, wdn_ref,
+    mask_hbm, x_hbm, cot_hbm, gin_hbm, win_hbm, gmid_hbm, wout_hbm, gtr_hbm, wup_hbm, wdn_hbm,
     up_ref, grad_ref,
+    mask_ref, x_ref, cot_ref, gin_ref, win_ref, gmid_ref, wout_ref, gtr_ref, wup_ref, wdn_ref, in_sem,
     r_all, l_all, rt, l_row, dc_row, dc_col,
     mask_v, hat_v, inv_v, proj_v, own_v, a_v, b_v, dleft_v, dright_v, dcar_v, dgate_v,
     s_send, s_recv,
@@ -78,6 +79,17 @@
             barrier, inc=1, device_id={"col": lax.rem(col + s, peers)}, device_id_type=MESH
         )
 
+    ins = [
+        pltpu.make_async_copy(src, dst, in_sem.at[n])
+        for n, (src, dst) in enumerate((
+            (mask_hbm, mask_ref), (x_hbm, x_ref), (gin_hbm, gin_ref), (win_hbm, win_ref),
+            (cot_hbm, cot_ref), (gmid_hbm, gmid_ref), (wout_hbm, wout_ref), (gtr_hbm, gtr_ref),
+            (wup_hbm, wup_ref), (wdn_hbm, wdn_ref),
+        ))
+    ]
+    for load in ins:
+        load.start()
+
     def copy(kind, src, dst, slot, axis, peer, lane=None):
         return pltpu.make_async_remote_copy(
             src_ref=src, dst_ref=dst,
@@ -109,20 +121,20 @@
         d = part(r_all, src, p)
         return copy(5 + m, d, d, src, "row", peer)
 
-    def dc_over_rows(src, slot, peer):
-        return copy(9, dc_row.at[src], dc_col.at[slot], slot, "row", peer)
+    def dc_over_rows(src, slot, peer, n):
+        return copy(16 + n, dc_row.at[src, chunks[n]], dc_col.at[slot, chunks[n]], slot, "row", peer)
 
     def along(kind, ref, tile, n, up):
         d = ref.at[tile, chunks[n]]
         peer = col + 1 if up else col - 1
-        return copy(kind + n, d, d, tile, "col", peer, lane=kind + n + (0 if up else 6))
+        return copy(kind + n, d, d, tile, "col", peer, lane=kind + n + (0 if up else 9))
 
     def pass_on(kind, ref, tile, n, up):
         @pl.when((col + 1 < peers) if up else (col > 0))
         def _():
             along(kind, ref, tile, n, up).start()
 
-    def forward(kind, ref, s):
+    def forward(kind, ref, s, then=None):
         for n in range(len(chunks)):
             for up in (True, False):
                 tile = col - s if up else col + s
@@ -131,6 +143,8 @@
                 def _():
                     along(kind, ref, tile, n, not up).wait_recv()
                     pass_on(kind, ref, tile, n, up)
+                    if then is not None:
+                        then(tile, n)
 
     def both(s, body):
         @pl.when(col - s >= 0)
@@ -153,6 +167,9 @@
     def wait_rest(src):
         for m in range(1, PIECES):
             rest(src, m, lax.rem(mine + m, PIECES), src).wait_recv()
+
+    for load in ins[:4]:
+        load.wait()
 
     at_k = lax.broadcasted_iota(jnp.int32, (t, c), 0)
     m_k = jnp.zeros((t, c), F32)
@@ -172,15 +189,6 @@
         proj_v[at, 3 * c : 4 * c] = gate
         r_all[row, at, :] = (mask_v[at, :] * gate * pr[:, :c]).astype(BF16)
 
-    pl.semaphore_wait(barrier, 2 * (peers - 1))
-
-    def send_r(s, _):
-        peer = lax.rem(row + s, peers)
-        first(row, peer, lax.rem(peer, PIECES)).start()
-        return 0
-
-    lax.fori_loop(1, peers, send_r, 0)
-
     for n, at in enumerate(chunks):
         normed = (hat_v[at, :] * gin_ref[...]).astype(BF16)
         pr = nn(normed, win_ref[:, : 2 * c])
@@ -189,9 +197,20 @@
         proj_v[at, c : 2 * c] = gate
         left = (mask_v[at, :] * gate * pr[:, :c]).astype(BF16)
         l_row[col, at, :] = left
+        l_all[row, at, :] = left
+
+    pl.semaphore_wait(barrier, 2 * (peers - 1))
+
+    def send_r(s, _):
+        peer = lax.rem(row + s, peers)
+        first(row, peer, lax.rem(peer, PIECES)).start()
+        return 0
+
+    lax.fori_loop(1, peers, send_r, 0)
+
+    for n in range(len(chunks)):
         for up in (True, False):
             pass_on(10, l_row, col, n, up)
-        l_all[row, at, :] = left
 
     def piece_step(s, _):
         src = lax.rem(row - s + peers, peers)
@@ -244,12 +263,26 @@
             a_v[at, :] = l_row[slot, at, :].astype(F32)
         products(t, a_v, lambda p, k: p * t + k, b_v, lambda k: pl.ds(k, t, stride=t), own_v, True)
 
+    def send_l(s, _):
+        left_over_rows(row, lax.rem(row + s, peers)).start()
+        return 0
+
     def forward_step(s, _):
         forward(10, l_row, s)
-        both(s, share)
 
         @pl.when(s == 1)
         def _():
+            def share_step(d, _):
+                both(d, share)
+                return 0
+
+            lax.fori_loop(1, peers, share_step, 0)
+
+            @pl.when(row != col)
+            def _():
+                start_rest()
+
+            lax.fori_loop(1, peers, send_l, 0)
             combine(col)
 
         @pl.when(s > 1)
@@ -259,17 +292,10 @@
         return 0
 
     lax.fori_loop(1, peers, forward_step, 0)
-
-    @pl.when(row != col)
-    def _():
-        start_rest()
-
-    def send_l(s, _):
-        left_over_rows(row, lax.rem(row + s, peers)).start()
-        return 0
-
-    lax.fori_loop(1, peers, send_l, 0)
     both(peers - 1, combine)
+
+    for load in ins[4:]:
+        load.wait()
 
     for n, at in enumerate(chunks):
         hat, inv = ln(own_v[at, :])
@@ -296,14 +322,14 @@
         dleft_v[at, :] = jnp.zeros((step, c), F32)
         dright_v[at, :] = jnp.zeros((step, c), F32)
 
-    def hand_on(tile):
+    def hand_on(tile, n):
         @pl.when(tile == row)
         def _():
-            dc_col[row] = dc_row[tile]
+            dc_col[row, chunks[n], :] = dc_row[tile, chunks[n], :]
 
         @pl.when(tile != row)
         def _():
-            dc_over_rows(tile, row, tile).start()
+            dc_over_rows(tile, row, tile, n).start()
 
     def to_left(tile):
         @pl.when((tile != row) & (tile != col))
@@ -315,24 +341,8 @@
             b_v[at, :] = r_all[tile, at, :].astype(F32)
         products(t, a_v, lambda p, j: p * t + j, b_v, lambda j: pl.ds(j * t, t), dleft_v, True)
 
-    hand_on(col)
-
-    def back_step(s, _):
-        forward(13, dc_row, s)
-        both(s, hand_on)
-
-        @pl.when(s == 1)
-        def _():
-            to_left(col)
-
-        @pl.when(s > 1)
-        def _():
-            both(s - 1, to_left)
-
-        return 0
-
-    lax.fori_loop(1, peers, back_step, 0)
-    both(peers - 1, to_left)
+    for n in range(len(chunks)):
+        hand_on(col, n)
 
     def right_step(s, _):
         src = lax.rem(row - s + peers, peers)
@@ -340,7 +350,8 @@
         @pl.when(s > 0)
         def _():
             left_over_rows(src, src).wait_recv()
-            dc_over_rows(src, src, src).wait_recv()
+            for n in range(len(chunks)):
+                dc_over_rows(src, src, src, n).wait_recv()
 
         for at in chunks:
             a_v[at, :] = dc_col[src, at, :].astype(F32)
@@ -348,7 +359,23 @@
         products(t, a_v, lambda p, i: i * t + p, b_v, lambda i: pl.ds(i * t, t), dright_v, True)
         return 0
 
+    def back_step(s, _):
+        forward(13, dc_row, s, hand_on)
+
+        @pl.when(s == 1)
+        def _():
+            to_left(col)
+
+        @pl.when(s > 1)
+        def _():
+            both(s - 1, to_left)
+
+        return 0
+
+    lax.fori_loop(1, peers, back_step, 0)
+    both(peers - 1, to_left)
     lax.fori_loop(0, peers, right_step, 0)
+
 
     for at in chunks:
         total = None
@@ -371,7 +398,8 @@
             left_over_rows(row, tile).wait_send()
             for m in range(1, PIECES):
                 rest(row, m, mine, tile).wait_send()
-            dc_over_rows(tile, row, tile).wait_send()
+            for n in range(len(chunks)):
+                dc_over_rows(tile, row, tile, n).wait_send()
 
         @pl.when(tile != col)
         def _():
@@ -402,27 +430,31 @@
     rows = t * t
     step = rows // 3
     tile, tile_all = (rows, c), (peers, rows, c)
+    args = (
+        residue_mask, pair_map.reshape(tile), cotangent.reshape(tile), gain_in[None], w_in,
+        gain_mid[None], w_out, gain_trans[None], w_up, w_down,
+    )
     vmem = pl.BlockSpec(memory_space=pltpu.VMEM)
     up, grad = pl.pallas_call(
         functools.partial(kernel, peers, t, step),
         out_shape=[jax.ShapeDtypeStruct(tile, BF16)] * 2,
-        in_specs=[pl.BlockSpec(memory_space=pltpu.SMEM)] + [vmem] * 9,
+        in_specs=[pl.BlockSpec(memory_space=pltpu.HBM)] * 10,
         out_specs=[vmem] * 2,
-        scratch_shapes=[pltpu.VMEM(tile_all, BF16)] * 6
+        scratch_shapes=[pltpu.SMEM(args[0].shape, jnp.int32)]
+        + [pltpu.VMEM(a.shape, a.dtype) for a in args[1:]]
+        + [pltpu.SemaphoreType.DMA((len(args),))]
+        + [pltpu.VMEM(tile_all, BF16)] * 6
         + [pltpu.VMEM(tile, F32)] * 3
         + [pltpu.VMEM((rows, w_in.shape[1]), F32)]
         + [pltpu.VMEM(tile, F32)] * 7
         + [
-            pltpu.SemaphoreType.DMA((22, peers)),
-            pltpu.SemaphoreType.DMA((16, peers)),
+            pltpu.SemaphoreType.DMA((25, peers)),
+            pltpu.SemaphoreType.DMA((19, peers)),
         ],
         compiler_params=pltpu.CompilerParams(
-            collective_id=0, has_side_effects=True, vmem_limit_bytes=48 * 1024 * 1024
+            collective_id=0, has_side_effects=True, vmem_limit_bytes=63 * 1024 * 1024
         ),
-    )(
-        residue_mask, pair_map.reshape(tile), cotangent.reshape(tile), gain_in[None], w_in,
-        gain_mid[None], w_out, gain_trans[None], w_up, w_down,
-    )
+    )(*args)
     return up.reshape(pair_map.shape), grad.reshape(pair_map.shape)
 
 

time: 51.6 us -> 44.5 us (0.86)
  local copies, waits for them, and re-layouts: 7.29 us -> 2.29 us
  Pallas kernels: 43.3 us -> 41.5 us
    unnamed x22 -> x4, local copies, waits for them, and re-layouts: 7.29 us -> 2.29 us
    pallas_call x1, Pallas kernels: 43.3 us -> 41.5 us  [shards(): pl.pallas_call(functools.partial(kernel, peers, t, step), out_shape=[jax....]
where the time goes in v2:
time: 44.5 us; the launch traced here: 44.4 us
  Pallas kernels  41.5 us (93%)
  local copies, waits for them, and re-layouts  2.29 us (5%)
  between operations  0.65 us (1%)
    pallas_call x1, Pallas kernels, shards(): pl.pallas_call(functools.partial(kernel, peers, t, step), out_shape=[jax....  41.5 us
    unnamed x4, local copies, waits for them, and re-layouts  2.29 us

profile of v2, /device:TPU:0, one launch (start us, length us, event | category | flops | bytes accessed | tf_op | source)
XLA Modules:
  0.0 44.4 jit_solution(5159730534759437933)
XLA Ops:
  0.6 41.5 %shard_map.113 = (bf16[576,128]{1,0:T(8,128)(2,1)}, bf16[576,128]{1,0:T(8,128)(2,1)}) custom-call(s32[96]{0:T(128)} %mask_hbm.1, bf16[576,128]{1,0:T(8,128)(2,1)} %bitcast.9, bf16[576,128]{1,0:T(8,128)(2,1)} %bitcast.10, f32[1,128]{1,0:T(1,128)} %bitcast.11, bf16[128,640]{1,0:T(8,128)(2,1)} %win_hbm.1, f32[1,128]{1,0:T(1,128)} %bitcast.12, ...), custom_call_target="tpu_custom_call" | custom-call | tf_op jit(solution)/shard_map/pallas_call | solution.py:438
  42.1 0.0 copy-start
  42.1 1.6 %copy.14 = bf16[24,24,128]{2,1,0:T(8,128)(2,1)} copy(bf16[24,24,128]{2,1,0:T(8,128)(2,1)} %bitcast.8) | data formatting | bytes 294912
  43.7 0.0 copy-done
  43.7 0.7 %copy.15 = bf16[24,24,128]{2,1,0:T(8,128)(2,1)} copy(bf16[24,24,128]{2,1,0:T(8,128)(2,1)S(1)} %bitcast.7) | data formatting | bytes 294912
Async XLA Ops:
  42.1 1.6 %copy-start = (bf16[576,128]{1,0:T(8,128)(2,1)S(1)}, bf16[576,128]{1,0:T(8,128)(2,1)}, u32[]{:S(2)}) copy-start(bf16[576,128]{1,0:T(8,128)(2,1)} %get-tuple-element.5) | copy-start | bytes 442372
